TPU v7x, 256 devices: a whole 4x4x8 slice. The times are simulated.
256 devices in a mesh: dp: 8 (over y, core), seq: 32 (over x, z).
Axes of the slice: x: 4, y: 4, z: 8, core: 2. Of those that a mesh axis runs over, the one named last changes fastest.
Arguments:
- xbc: bfloat16 [131072, 4352], P(('dp', 'seq')), parts along dimension 0, may hold values from -6 to 6
- dt_raw: bfloat16 [131072, 64], P(('dp', 'seq')), parts along dimension 0, may hold values from -2.3 to 2.3
- conv_weight: float32 [4, 4352], replicated, may hold values from -3 to 3
- conv_bias: float32 [4352], replicated, may hold values from -1.5 to 1.5
- dt_bias: float32 [64], replicated, may hold values from -4 to -2
- a_log: float32 [64], replicated, may hold values from -8.6 to -0.2
- d_skip: float32 [64], replicated, may hold values from 0.5 to 2
- doc_lengths: int32 [128], P('dp'), parts along dimension 0, may hold values from 1 to 4096, 16384 in all
- loader_dest: int32 [1024], P('dp'), parts along dimension 0, may hold values from 0 to 127, as said below
Outputs:
- layer_out: bfloat16 [131072, 4096], P(('dp', 'seq')), parts along dimension 0
There are 8 independent parts, one for each index of `dp`. A program takes and returns all parts, laid end to end along the dimension named above; an argument that names none is the same for every part. Nothing has to cross between parts.
Inputs may be any that keep to these rules, and one draw needn't show every extreme that they name: `loader_dest`: a permutation of the block numbers; the loader block at index b lies on seq device b // 4 and goes to a sequence block on a device at most 2 steps away along seq, counted around the axis; every device sends blocks to exactly four of the five devices within that reach (itself among the five), and exactly 1 block to each of the four. `doc_lengths`: they sum to 16384.
All inputs are finite; a program needn't handle non-finite values.
Results may differ from a plain program's by a relative error of at most 0.006.
Values may be sent and summed in bfloat16 or wider, within the bound.
A program may use at most 256 MiB of HBM per device.

v0:
```python
import jax
import jax.numpy as jnp
from jax import lax
from jax.sharding import PartitionSpec as P

P_SIZE = 64
NS = 128
GROUP = 256
KW = 4
BLOCK_ROWS = 128


def passed_along(value, axis, steps):
    count = lax.axis_size(axis)
    pairs = [(source, (source + steps) % count) for source in range(count)]
    return lax.ppermute(value, axis, pairs)


def from_behind(block, axis, distance):
    devices = range(lax.axis_size(axis))
    route = [(i - distance, i) for i in devices if i - distance in devices]
    return lax.ppermute(block, axis, route)


def entering(value, axis, join, neutral):
    count, mine = (lax.axis_size(axis), lax.axis_index(axis))
    pieces = jax.tree.map(lambda part: lax.all_gather(part, axis), value)
    running = jax.tree.map(
        lambda part, zero: jnp.full_like(part, 0) + jnp.asarray(zero, part.dtype), value, neutral
    )

    def turn(position, running):
        longer = join(running, jax.tree.map(lambda part: part[position], pieces))
        return jax.tree.map(lambda new, old: jnp.where(position < mine, new, old), longer, running)

    return lax.fori_loop(0, count - 1, turn, running)


def document_ids(doc_lengths, positions):
    ends = jnp.cumsum(doc_lengths)
    starts = ends - doc_lengths
    return jnp.sum((starts[None, :] <= positions[:, None]).astype(jnp.int32), axis=1) - 1


def routed(targets, dest, per_dev, per_pair):
    chosen = targets // per_dev == dest
    picks = jnp.nonzero(chosen, size=per_pair, fill_value=0)[0]
    filled = jnp.arange(per_pair) < jnp.sum(chosen.astype(jnp.int32))
    slots = jnp.where(filled, targets[picks] % per_dev, per_dev)
    return (picks, slots)


def state_product(cpart, state):
    upper = state.astype(jnp.bfloat16)
    lower = (state - upper.astype(jnp.float32)).astype(jnp.bfloat16)
    first = jnp.einsum("tn,hpn->thp", cpart, upper, preferred_element_type=jnp.float32)
    return first + jnp.einsum("tn,hpn->thp", cpart, lower, preferred_element_type=jnp.float32)


def group_pieces(xpart, bpart, cpart, dtpart, ratepart, docpart, prev_doc):
    length = xpart.shape[0]
    heads = dtpart.shape[1]
    cum = jnp.cumsum(ratepart, axis=0)
    scores = jnp.dot(cpart, bpart.T, preferred_element_type=jnp.float32)
    order = jnp.arange(length, dtype=jnp.int32)
    same = (docpart[:, None] == docpart[None, :]) & (order[None, :] <= order[:, None])
    gap = jnp.minimum(cum[:, None, :] - cum[None, :, :], 0.0)
    weight = jnp.where(
        same[:, :, None], scores[:, :, None] * jnp.exp(gap) * dtpart[None, :, :], 0.0
    ).astype(jnp.bfloat16)
    values = xpart.reshape(length, heads, -1)
    intra = jnp.einsum("tsh,shp->thp", weight, values, preferred_element_type=jnp.float32)
    last = length - 1
    tail = docpart == docpart[last]
    end_weight = jnp.where(tail[:, None], jnp.exp(cum[last][None, :] - cum) * dtpart, 0.0)
    scaled_b = (end_weight[:, :, None] * bpart.astype(jnp.float32)[:, None, :]).astype(jnp.bfloat16)
    state = jnp.einsum("shn,shp->hpn", scaled_b, values, preferred_element_type=jnp.float32)
    into = jnp.where((docpart == prev_doc)[:, None], jnp.exp(cum), 0.0)
    decay = jnp.where(docpart[last] == prev_doc, jnp.exp(cum[last]), 0.0)
    return (intra, state, into, decay, values)


def link_states(earlier, later):
    return (earlier[0] * later[0], later[0][:, None, None] * earlier[1] + later[1])


def body(xbc, dt_raw, conv_weight, conv_bias, dt_bias, a_log, d_skip, doc_lengths, loader_dest):
    rows, width = xbc.shape
    heads = dt_raw.shape[1]
    inner = heads * P_SIZE
    per_dev = rows // BLOCK_ROWS
    per_pair = per_dev // 4
    devices = lax.axis_size("seq")
    me = lax.axis_index("seq")
    blocks = xbc.reshape(per_dev, BLOCK_ROWS, width)
    dt_blocks = dt_raw.reshape(per_dev, BLOCK_ROWS, heads)
    mine = lax.dynamic_slice_in_dim(loader_dest, me * per_dev, per_dev)
    picks, slots = routed(mine, me, per_dev, per_pair)
    placed = jnp.zeros_like(blocks).at[slots].set(blocks[picks], mode="drop")
    placed_dt = jnp.zeros_like(dt_blocks).at[slots].set(dt_blocks[picks], mode="drop")
    for offset in (-2, -1, 1, 2):
        out_picks, unused = routed(mine, (me + offset) % devices, per_dev, per_pair)
        got_rows, got_steps = passed_along((blocks[out_picks], dt_blocks[out_picks]), "seq", offset)
        source = (me - offset) % devices
        theirs = lax.dynamic_slice_in_dim(loader_dest, source * per_dev, per_dev)
        unused_picks, in_slots = routed(theirs, me, per_dev, per_pair)
        placed = placed.at[in_slots].set(got_rows, mode="drop")
        placed_dt = placed_dt.at[in_slots].set(got_steps, mode="drop")
    seq_x = placed.reshape(rows, width)
    seq_dt = placed_dt.reshape(rows, heads)
    start = me * rows
    docs = document_ids(doc_lengths, start + jnp.arange(rows, dtype=jnp.int32))
    rim = from_behind(seq_x[rows - (KW - 1) :], "seq", 1)
    extended = jnp.concatenate([rim, seq_x], axis=0)
    ext_docs = document_ids(
        doc_lengths, start - (KW - 1) + jnp.arange(rows + KW - 1, dtype=jnp.int32)
    )
    conv = jnp.zeros((rows, width), jnp.float32) + conv_bias[None, :]
    for back in range(KW):
        lead = KW - 1 - back
        piece = extended[lead : lead + rows]
        keep = ext_docs[lead : lead + rows] == docs
        conv = conv + jnp.where(
            keep[:, None], conv_weight[KW - 1 - back][None, :] * piece.astype(jnp.float32), 0.0
        )
    mixed = jax.nn.silu(conv).astype(jnp.bfloat16)
    xval = mixed[:, :inner]
    bmat = mixed[:, inner : inner + NS]
    cmat = mixed[:, inner + NS :]
    dt = jax.nn.softplus(seq_dt.astype(jnp.float32) + dt_bias[None, :])
    rate = -jnp.exp(a_log)[None, :] * dt
    count = rows // GROUP
    prev_docs = document_ids(doc_lengths, start - 1 + GROUP * jnp.arange(count, dtype=jnp.int32))

    def advance(carry, pieces):
        local_state, through = carry
        xpart, bpart, cpart, dtpart, ratepart, docpart, prev_doc = pieces
        intra, state, into, decay, values = group_pieces(
            xpart, bpart, cpart, dtpart, ratepart, docpart, prev_doc
        )
        carried = state_product(cpart, local_state)
        partial_value = (
            intra + into[:, :, None] * carried + d_skip[None, :, None] * values.astype(jnp.float32)
        )
        return (
            (decay[:, None, None] * local_state + state, through * decay),
            (partial_value, into * through[None, :]),
        )

    begin = (jnp.zeros((heads, P_SIZE, NS), jnp.float32), jnp.ones((heads,), jnp.float32))
    (end_state, end_decay), (partials, scales) = lax.scan(
        advance,
        begin,
        (
            xval.reshape(count, GROUP, inner),
            bmat.reshape(count, GROUP, NS),
            cmat.reshape(count, GROUP, NS),
            dt.reshape(count, GROUP, heads),
            rate.reshape(count, GROUP, heads),
            docs.reshape(count, GROUP),
            prev_docs,
        ),
    )
    identity = (jnp.ones_like(end_decay), jnp.zeros_like(end_state))
    unused_decay, incoming = entering((end_decay, end_state), "seq", link_states, identity)
    correction = state_product(cmat, incoming)
    total = (
        partials.reshape(rows, heads, P_SIZE) + scales.reshape(rows, heads)[:, :, None] * correction
    )
    return total.reshape(rows, inner).astype(jnp.bfloat16)


def solution(mesh):
    placed = (
        P(("dp", "seq"), None),
        P(("dp", "seq"), None),
        P(),
        P(),
        P(),
        P(),
        P(),
        P("dp"),
        P("dp"),
    )
    return jax.shard_map(
        body, mesh=mesh, in_specs=placed, out_specs=P(("dp", "seq"), None), check_vma=False
    )
```

profile of v0, /device:TPU:1, one launch (start us, length us, event | category | flops | bytes accessed | tf_op | source)
XLA Modules:
  0.0 969.7 jit_solution(13343602508677827363)
XLA Ops:
  55.5 5.5 constant_dynamic-slice_fusion.4
  61.0 9.1 collective-permute-start.4
  73.4 5.3 collective-permute-start
  92.8 50.3 %collective-permute-done = bf16[1,128,64]{1,0,2:T(2,128)(2,1)} collective-permute-done((bf16[1,128,64]{1,0,2:T(2,128)(2,1)}, bf16[1,128,64]{1,0,2:T(2,128)(2,1)}, u32[]{:S(2)}, u32[]{:S(2)}) %collective-permute-start) | collective-permute-done | bytes 16416 | tf_op jit(solution)/shard_map/ppermute | solution.py:16
  143.1 3.5 collective-permute-start.1
  149.8 4.5 collective-permute-done.2
  155.2 6.1 collective-permute-done.3
  162.3 3.5 select_dynamic-update-slice_fusion.3
  165.7 3.5 select_dynamic-update-slice_fusion.2
  169.3 3.5 select_dynamic-update-slice_fusion.1
  172.8 3.5 select_dynamic-update-slice_fusion
  179.5 14.7 %multiply_convert_fusion.4 = bf16[512,4352]{1,0:T(8,128)(2,1)S(1)} fusion(bf16[512,4352]{1,0:T(8,128)(2,1)} %bitcast.48, bf16[3,4352]{1,0:T(4,128)(2,1)S(1)} %collective-permute-done.8, f32[4352]{0:T(1024)S(1)} %copy-done.5, f32[4352]{0:T(1024)S(1)} %copy-done.6, f32[4352]{0:T(1024)S(1)} %copy-done.4, f32[4352]{0:T(1024)S(1)} %copy-done.3, ...), kind=kLoop, calls=%fused_computation.72 | loop fusion | flops 66846720 | bytes 9028096 | tf_op jit(solution)/shard_map/convert_element_type | solution.py:126
  194.2 3.0 slice.391
  197.5 250.1 %while.58 = (s32[]{:T(128)}, f32[64,64,128]{2,1,0:T(8,128)S(1)}, f32[64]{0:T(128)S(1)}, f32[2,256,64,64]{1,0,3,2:T(2,128)}, f32[2,256,64]{1,0,2:T(2,128)S(1)}, /...) while((s32[]{:T(128)}, f32[64,64,128]{2,1,0:T(8,128)S(1)}, ...), condition=%wide.region_39.40_spmd.clone.clone, body=%wide.region_36.39_spmd.clone.sunk.clone | while | flops 1401750400 | bytes 78394624 | solution.py:151
  205.4 2.8 fusion.108
  210.3 4.1 copy.101
  214.4 9.3 fusion.111
  223.7 8.9 copy.103
  232.6 84.3 %dynamic_update_slice.14 = f32[2,256,64,64]{1,0,3,2:T(2,128)} dynamic-update-slice(f32[2,256,64,64]{1,0,3,2:T(2,128)} %get-tuple-element.896, f32[1,256,64,64]{1,0,3,2:T(1,128)} %copy.103, s32[]{:T(128)} %get-tuple-element.893, s32[]{:T(128)} %constant.604.clone.1..sunk.2, s32[]{:T(128)} %constant.604.clone.1..sunk.2, s32[]{:T(128)} %constant.604.clone.1..sunk.2) | dynamic-update-slice | bytes 8388612 | tf_op jit(solution)/shard_map/while/body/jit(dynamic_update_index_in_dim)/dynamic_update_slice | solution.py:151
  317.0 4.6 multiply_add_fusion.4
  330.5 2.8 fusion.108
  335.4 4.1 copy.101
  339.5 9.3 fusion.111
  348.8 8.9 copy.103
  357.7 84.3 %dynamic_update_slice.14 = f32[2,256,64,64]{1,0,3,2:T(2,128)} dynamic-update-slice(f32[2,256,64,64]{1,0,3,2:T(2,128)} %get-tuple-element.896, f32[1,256,64,64]{1,0,3,2:T(1,128)} %copy.103, s32[]{:T(128)} %get-tuple-element.893, s32[]{:T(128)} %constant.604.clone.1..sunk.2, s32[]{:T(128)} %constant.604.clone.1..sunk.2, s32[]{:T(128)} %constant.604.clone.1..sunk.2) | dynamic-update-slice | bytes 8388612 | tf_op jit(solution)/shard_map/while/body/jit(dynamic_update_index_in_dim)/dynamic_update_slice | solution.py:151
  442.0 4.6 multiply_add_fusion.4
  450.6 60.6 %all-reduce = f32[2048]{0:T(1024)S(1)} all-reduce(f32[2048]{0:T(1024)S(1)} %dynamic-update-slice.45), channel_id=2, replica_groups=mesh['dp'=8,'seq'=32] {'seq'}, use_global_device_ids=true, to_apply=%add | all-reduce | flops 2048 | bytes 16384
  511.3 11.7 %reshape.807 = f32[512,64,64]{0,2,1:T(8,128)} reshape(f32[2,256,64,64]{1,0,3,2:T(2,128)} %get-tuple-element.289) | data formatting | bytes 16777216 | tf_op jit(solution)/shard_map/reshape | solution.py:168
  523.1 359.9 %all-gather.4.cloned.1.call-done = f32[2048,64,128]{2,1,0:T(8,128)} async-done(((f32[64,64,128]{2,1,0:T(8,128)}), f32[2048,64,128]{2,1,0:T(8,128)}) %all-gather.4.cloned.1.call-update) | async-done | bytes 67108880 | tf_op jit(solution)/shard_map/all_gather | solution.py:27
  883.0 65.8 %while.59 = (s32[]{:T(128)}, f32[64,64,128]{2,1,0:T(8,128)S(1)}, s32[]{:T(128)}, f32[32,64]{1,0:T(8,128)S(1)}, f32[32,64,64,128]{3,2,1,0:T(8,128)}) while((s32[]{:T(128)}, f32[64,64,128]{2,1,0:T(8,128)S(1)}, s32[]{:T(128)}, f32[32,64]{1,0:T(8,128)S(1)}, f32[32,64,64,128]{3,2,1,0:T(8,128)}) %tuple.242), condition=%wide.region_41.42_spmd.clone.clone, body=%wide.region_40.41_spmd.clone.sunk.clone | while | flops 2097156 | bytes 6292313 | solution.py:36
  952.3 4.2 add_convert_fusion
  956.5 6.3 copy.60
  (245 shorter events, 129.1 us)
Async XLA Ops:
  6.5 25.6 %copy-start.9 = (s32[128]{0:T(128)S(1)}, s32[128]{0:T(128)}, u32[]{:S(2)}) copy-start(s32[128]{0:T(128)} %param.41) | copy-start | bytes 1540
  6.5 876.4 %all-gather.4.cloned.1.call-start = ((), (), s32[]{:S(2)}) async-start(), calls=%async_computation | async-start | bytes 69206016 | tf_op jit(solution)/shard_map/all_gather | solution.py:27
  13.8 38.5 %copy-start.13 = (s32[3]{0:T(128)S(1)}, s32[3]{0:T(128)}, u32[]{:S(2)}) copy-start(s32[3]{0:T(128)} %constant.620.clone.1) | copy-start | bytes 40
  55.5 16.5 %copy-start.8 = (bf16[512,64]{0,1:T(8,128)(2,1)S(1)}, bf16[512,64]{0,1:T(8,128)(2,1)}, u32[]{:S(2)}) copy-start(bf16[512,64]{0,1:T(8,128)(2,1)} %param.34) | copy-start | bytes 196612
  55.5 33.2 %copy-start.16 = (s32[16]{0:T(128)S(1)}, s32[16]{0:T(128)}, u32[]{:S(2)}) copy-start(s32[16]{0:T(128)} %param.40) | copy-start | bytes 196
  55.5 34.3 %copy-start.17 = (f32[64]{0:T(128)S(1)}, f32[64]{0:T(128)}, u32[]{:S(2)}) copy-start(f32[64]{0:T(128)} %param.38) | copy-start | bytes 772
  55.5 35.6 %copy-start.7 = (f32[4,4352]{1,0:T(4,128)S(1)}, f32[4,4352]{1,0:T(4,128)}, u32[]{:S(2)}) copy-start(f32[4,4352]{1,0:T(4,128)} %param.35) | copy-start | bytes 208900
  61.0 101.3 %collective-permute-start.4 = (bf16[1,128,4352]{2,1,0:T(8,128)(2,1)}, bf16[1,128,4352]{2,1,0:T(8,128)(2,1)}, u32[]{:S(2)}, u32[]{:S(2)}) collective-permute-start(bf16[1,128,4352]{2,1,0:T(8,128)(2,1)} %get-tuple-element.660), channel_id=1, source_target_pairs={{0,30},{1,31},{2,0},{3,1},{4,2},{5,3},{6,4},{7,5},{8,6},{9,7},{10,... | collective-permute-start | bytes 3342344 | tf_op jit(solution)/shard_map/ppermute | solution.py:16
  70.1 95.7 %collective-permute-start.5 = (bf16[1,128,4352]{2,1,0:T(8,128)(2,1)}, bf16[1,128,4352]{2,1,0:T(8,128)(2,1)}, u32[]{:S(2)}, u32[]{:S(2)}) collective-permute-start(bf16[1,128,4352]{2,1,0:T(8,128)(2,1)} %get-tuple-element.659), channel_id=1, source_target_pairs={{0,31},{1,0},{2,1},{3,2},{4,3},{5,4},{6,5},{7,6},{8,7},{9,8},{10,9... | collective-permute-start | bytes 3342344 | tf_op jit(solution)/shard_map/ppermute | solution.py:16
  70.8 98.5 %collective-permute-start.6 = (bf16[1,128,4352]{2,1,0:T(8,128)(2,1)}, bf16[1,128,4352]{2,1,0:T(8,128)(2,1)}, u32[]{:S(2)}, u32[]{:S(2)}) collective-permute-start(bf16[1,128,4352]{2,1,0:T(8,128)(2,1)} %get-tuple-element.658), channel_id=1, source_target_pairs={{0,1},{1,2},{2,3},{3,4},{4,5},{5,6},{6,7},{7,8},{8,9},{9,10},{10,1... | collective-permute-start | bytes 3342344 | tf_op jit(solution)/shard_map/ppermute | solution.py:16
  71.5 101.2 %collective-permute-start.7 = (bf16[1,128,4352]{2,1,0:T(8,128)(2,1)S(1)}, bf16[1,128,4352]{2,1,0:T(8,128)(2,1)}, u32[]{:S(2)}, u32[]{:S(2)}) collective-permute-start(bf16[1,128,4352]{2,1,0:T(8,128)(2,1)S(1)} %get-tuple-element.657), channel_id=1, source_target_pairs={{0,2},{1,3},{2,4},{3,5},{4,6},{5,7},{6,8},{7,9},{8,10},{9,11},{10,... | collective-permute-start | bytes 3342344 | tf_op jit(solution)/shard_map/ppermute | solution.py:16
  73.4 69.7 %collective-permute-start = (bf16[1,128,64]{1,0,2:T(2,128)(2,1)}, bf16[1,128,64]{1,0,2:T(2,128)(2,1)}, u32[]{:S(2)}, u32[]{:S(2)}) collective-permute-start(bf16[1,128,64]{1,0,2:T(2,128)(2,1)} %get-tuple-element.665), channel_id=1, source_target_pairs={{0,30},{1,31},{2,0},{3,1},{4,2},{5,3},{6,4},{7,5},{8,6},{9,7},{10,... | collective-permute-start | bytes 49160 | tf_op jit(solution)/shard_map/ppermute | solution.py:16
  143.1 5.1 collective-permute-start.1
  148.2 6.2 collective-permute-start.2
  154.3 7.0 collective-permute-start.3
  169.2 9.4 copy-start.14
  169.2 9.4 copy-start.15
  169.2 10.3 %copy-start.3 = (f32[4352]{0:T(1024)S(1)}, f32[4352]{0:T(1024)}, u32[]{:S(2)}) copy-start(f32[4352]{0:T(1024)} %get-tuple-element.584) | copy-start | bytes 52228
  169.2 10.3 %copy-start.4 = (f32[4352]{0:T(1024)S(1)}, f32[4352]{0:T(1024)}, u32[]{:S(2)}) copy-start(f32[4352]{0:T(1024)} %get-tuple-element.585) | copy-start | bytes 52228
  169.2 10.3 %copy-start.5 = (f32[4352]{0:T(1024)S(1)}, f32[4352]{0:T(1024)}, u32[]{:S(2)}) copy-start(f32[4352]{0:T(1024)} %get-tuple-element.586) | copy-start | bytes 52228
  169.2 10.2 %copy-start.6 = (f32[4352]{0:T(1024)S(1)}, f32[4352]{0:T(1024)}, u32[]{:S(2)}) copy-start(f32[4352]{0:T(1024)} %get-tuple-element.587) | copy-start | bytes 52228
  169.2 10.2 %copy-start.10 = (f32[4352]{0:T(1024)S(1)}, f32[4352]{0:T(1024)}, u32[]{:S(2)}) copy-start(f32[4352]{0:T(1024)} %param.36) | copy-start | bytes 52228
  169.2 10.2 %copy-start.11 = (pred[512]{0:T(512)(128)(4,1)S(1)}, pred[512]{0:T(512)(128)(4,1)}, u32[]{:S(2)}) copy-start(pred[512]{0:T(512)(128)(4,1)} %get-tuple-element.669) | copy-start | bytes 1540
  169.3 10.2 %copy-start.12 = (pred[512]{0:T(512)(128)(4,1)S(1)}, pred[512]{0:T(512)(128)(4,1)}, u32[]{:S(2)}) copy-start(pred[512]{0:T(512)(128)(4,1)} %get-tuple-element.670) | copy-start | bytes 1540
  177.1 2.3 collective-permute-start.8
  194.2 3.4 copy-start.2
  194.2 3.3 copy-start.18
  194.2 3.3 copy-start.20
  197.5 251.5 %copy-start.19 = (u32[256]{0:T(256)S(1)}, u32[256]{0:T(256)}, u32[]{:S(2)}) copy-start(u32[256]{0:T(256)} %constant.945) | copy-start | bytes 3076
  205.4 3.5 copy-start.1
  330.5 3.5 copy-start.1
  948.8 3.5 slice-start.1
  (2 other events, 3.7 us)
Sparse Core Ops, SparseCore 0:
  449.2 433.7 all-gather.3
where the time goes:
time: 984 us; the launch traced here: 970 us
  waiting for transfers between devices  421 us (43%)
  local copies, waits for them, and re-layouts  235 us (24%)
  other arithmetic  132 us (13%)
  blocking collectives  60.6 us (6%)
  between operations  50.1 us (5%)
  matrix products  45.6 us (5%)
  starting transfers between devices  21.2 us (2%)
    all_gather x1, waiting for transfers between devices, entering(): pieces = jax.tree.map(lambda part: lax.all_gather(part, axis), value)  360 us
    dynamic_update_slice x8, local copies, waits for them, and re-layouts, body(): lax.scan(advance, begin, (xval.reshape(count, GROUP, inner), bmat.reshape...  188 us
    select_n x31, other arithmetic, turn(): jnp.where(position < mine, new, old)  64.4 us
    ppermute x8, waiting for transfers between devices, passed_along(): return lax.ppermute(value, axis, pairs)  60.9 us
    unnamed x1, blocking collectives  60.6 us
    ppermute x8, starting transfers between devices, passed_along(): return lax.ppermute(value, axis, pairs)  19.8 us
  transfers between devices with their start and end apart: 10, of which 5 were waited for; matrix products, arithmetic and copies ran while one was open for 4% of the time, Pallas kernels for 0%

commit v1 on v0

v1 whole, which is shorter than its diff:
```python
import functools

import jax
import jax.numpy as jnp
from jax import lax
from jax.experimental import pallas as pl
from jax.experimental.pallas import tpu as pltpu
from jax.sharding import PartitionSpec as P

P_SIZE = 64
NS = 128
KW = 4
BLOCK = 128
PER_DEV = 4
LINE = 8
HALO = 16
CHUNK = 512
OFFSETS = (-2, -1, 1, 2)
SLICE = NS // LINE
MESH = pl.DeviceIdType.MESH
F32 = jnp.float32
BF16 = jnp.bfloat16


def iota(shape, axis):
    return lax.broadcasted_iota(jnp.int32, shape, axis)


def chosen(which, options):
    value = options[0]
    for number, option in enumerate(options[1:], 1):
        value = lax.select(which == number, option, value)
    return value


def split_pack(value):
    high = value.astype(BF16).astype(F32)
    return jnp.where(iota(value.shape, 1) < 64, high, value - high).astype(BF16)


def kernel(
    devices, heads,
    lens, dest, x_hbm, dt_hbm, w_ref, b_ref, par_ref,
    out_hbm,
    xin, send, recv, dtin, dtsend, dtrecv, seqx, mixed, zbuf, loc, est, sbuf, runs,
    lsend, lrecv, isend, inc, ybuf, spread, shifts, lhs, btail, fac1, fac2, rowp, rowx,
    dmine, dline, dpack,
    in_sem, dt_sem, x_send, x_recv, d_send, d_recv, h_send, h_recv, t_send, t_recv,
    s_send, s_recv, l_send, l_recv, i_send, i_recv, out_sem,
):
    inner = heads * P_SIZE
    chunks = inner // CHUNK
    me = lax.axis_index("seq")
    z = lax.rem(me, LINE)
    base = me - z

    def at(offset):
        return lax.rem(me + offset + devices, devices)

    def cols(k):
        return pl.ds(pl.multiple_of(k * CHUNK, CHUNK), CHUNK)

    tail_cols = pl.ds(inner, 2 * NS)

    def load(k):
        return pltpu.make_async_copy(x_hbm.at[:, :, cols(k)], xin.at[:, :, cols(k)], in_sem.at[k])

    load_tail = pltpu.make_async_copy(x_hbm.at[:, :, tail_cols], xin.at[:, :, tail_cols], in_sem.at[chunks])
    load_dt = pltpu.make_async_copy(dt_hbm, dtin, dt_sem.at[0])
    load_dt.start()
    load_tail.start()

    def start_load(k, carry):
        load(k).start()
        return carry

    lax.fori_loop(0, chunks, start_load, 0)

    barrier = pltpu.get_barrier_semaphore()
    partners = [at(o) for o in OFFSETS] + [base + lax.rem(z + j, LINE) for j in range(1, LINE)] + [at(LINE), at(-LINE)]
    for partner in partners:
        pl.semaphore_signal(barrier, inc=1, device_id={"seq": partner}, device_id_type=MESH)

    reach = (-2, -1, 0, 1, 2)
    own = [lax.rem(lax.shift_right_logical(dest[me * PER_DEV + j], 2) - me + 2 + devices, devices) for j in range(PER_DEV)]
    picks = []
    for number in range(5):
        pick = jnp.int32(0)
        for j in range(1, PER_DEV):
            pick = pick + jnp.where(own[j] == number, j, 0)
        picks.append(pick)
    order = {-2: 0, -1: 1, 1: 2, 2: 3, 0: 4}
    origin = [jnp.int32(0) for _ in range(PER_DEV)]
    for offset in reach:
        source = at(-offset)
        for j in range(PER_DEV):
            target = dest[source * PER_DEV + j]
            for q in range(PER_DEV):
                origin[q] = origin[q] + jnp.where(target == me * PER_DEV + q, order[offset], 0)

    def exchange(k, o, where):
        return pltpu.make_async_remote_copy(
            src_ref=send.at[o, :, where], dst_ref=recv.at[o, :, where],
            send_sem=x_send.at[o, k], recv_sem=x_recv.at[o, k],
            device_id={"seq": at(OFFSETS[o])}, device_id_type=MESH)

    def exchange_dt(o):
        return pltpu.make_async_remote_copy(
            src_ref=dtsend.at[o], dst_ref=dtrecv.at[o],
            send_sem=d_send.at[o], recv_sem=d_recv.at[o],
            device_id={"seq": at(OFFSETS[o])}, device_id_type=MESH)

    def halo(k, where):
        return pltpu.make_async_remote_copy(
            src_ref=seqx.at[pl.ds(PER_DEV * BLOCK, HALO), where], dst_ref=seqx.at[pl.ds(0, HALO), where],
            send_sem=h_send.at[k], recv_sem=h_recv.at[k],
            device_id={"seq": at(1)}, device_id_type=MESH)

    def decay_copy(j):
        return pltpu.make_async_remote_copy(
            src_ref=dmine, dst_ref=dline.at[j],
            send_sem=t_send.at[j], recv_sem=t_recv.at[j],
            device_id={"seq": base + lax.rem(z + j, LINE)}, device_id_type=MESH)

    def state_copy(k, j):
        target = lax.rem(z + j, LINE)
        return pltpu.make_async_remote_copy(
            src_ref=est.at[k, pl.ds(pl.multiple_of(target * SLICE, SLICE), SLICE)], dst_ref=sbuf.at[k, j],
            send_sem=s_send.at[k, j], recv_sem=s_recv.at[k, j],
            device_id={"seq": base + target}, device_id_type=MESH)

    def line_copy(k):
        return pltpu.make_async_remote_copy(
            src_ref=lsend.at[k], dst_ref=lrecv.at[k],
            send_sem=l_send.at[k], recv_sem=l_recv.at[k],
            device_id={"seq": at(LINE)}, device_id_type=MESH)

    def back_copy(k, j):
        target = lax.rem(z + j, LINE)
        return pltpu.make_async_remote_copy(
            src_ref=isend.at[k, j], dst_ref=inc.at[k, pl.ds(pl.multiple_of(z * SLICE, SLICE), SLICE)],
            send_sem=i_send.at[k, j], recv_sem=i_recv.at[k, j],
            device_id={"seq": base + target}, device_id_type=MESH)

    def fill(where):
        blocks = [xin[j, :, where] for j in range(PER_DEV)]
        for o, offset in enumerate(OFFSETS):
            send[o, :, where] = chosen(picks[offset + 2], blocks)
        recv[4, :, where] = chosen(picks[2], blocks)

    def place(where):
        options = [recv[o, :, where] for o in range(5)]
        for q in range(PER_DEV):
            seqx[pl.ds(HALO + q * BLOCK, BLOCK), where] = chosen(origin[q], options)

    def send_chunk(k):
        load(k).wait()
        fill(cols(k))
        for o in range(4):
            exchange(k, o, cols(k)).start()

    load_dt.wait()
    dt_blocks = [dtin[j] for j in range(PER_DEV)]
    for o, offset in enumerate(OFFSETS):
        dtsend[o] = chosen(picks[offset + 2], dt_blocks)
    dtrecv[4] = chosen(picks[2], dt_blocks)
    load_tail.wait()
    fill(tail_cols)
    pl.semaphore_wait(barrier, len(partners))
    for o in range(4):
        exchange_dt(o).start()
        exchange(chunks, o, tail_cols).start()
    send_chunk(0)
    send_chunk(1)

    starts = []
    total = jnp.int32(0)
    for n in range(lens.shape[0]):
        starts.append(total)
        total = total + lens[n]

    def docs(positions):
        found = jnp.where(starts[0] <= positions, 0, -1)
        for begin in starts[1:]:
            found = found + jnp.where(begin <= positions, 1, 0)
        return found

    row = iota((BLOCK, BLOCK), 0)
    col = iota((BLOCK, BLOCK), 1)
    square = (BLOCK, BLOCK + HALO)

    def make_shift(q, carry):
        first = (me * PER_DEV + q) * BLOCK
        same = docs(iota(square, 0) + first) == docs(iota(square, 1) + (first - HALO))
        apart = iota(square, 1) - iota(square, 0)
        for j in range(1, KW):
            keep = same & (apart == HALO - j)
            shifts[q, pl.ds((j - 1) * BLOCK, BLOCK), :] = jnp.where(keep, 1.0, 0.0).astype(BF16)
        return carry

    lax.fori_loop(0, PER_DEV, make_shift, 0)

    def make_spread(k, carry):
        head = lax.shift_right_logical(iota((128, CHUNK), 1) + k * CHUNK, 6)
        match = (iota((128, CHUNK), 0) & 63) == head
        spread[:, cols(k)] = jnp.where(match, 1.0, 0.0).astype(BF16)
        return carry

    lax.fori_loop(0, chunks, make_spread, 0)

    double = jnp.where((iota((heads, 128), 1) & 63) == iota((heads, 128), 0), 1.0, 0.0)
    params = jnp.dot(par_ref[...], double, precision=lax.Precision.HIGHEST, preferred_element_type=F32)
    lower = jnp.where(col <= row, 1.0, 0.0)

    for o in range(4):
        exchange_dt(o).wait_recv()
    through = jnp.ones((1, 128), F32)
    dt_options = [dtrecv[o] for o in range(5)]
    rows = iota((16, 128), 0)
    packed = jnp.where(rows == 12, params[2:3], 0.0)
    for q in range(PER_DEV):
        raw = jnp.dot(chosen(origin[q], dt_options), double.astype(BF16), preferred_element_type=F32) + params[0:1]
        dt = jnp.maximum(raw, 0.0) + jnp.log1p(jnp.exp(-jnp.abs(raw)))
        rate = -jnp.exp(params[1:2]) * dt
        cum = jnp.dot(lower, rate, precision=lax.Precision.HIGHEST, preferred_element_type=F32)
        last = cum[BLOCK - 1 :, :]
        middle = 0.5 * last
        fac1[q] = split_pack(jnp.exp(cum - middle))
        fac2[q] = split_pack(jnp.exp(middle - cum) * dt)
        first = (me * PER_DEV + q) * BLOCK
        on = docs(first - 1) == docs(first + BLOCK - 1)
        decay = jnp.where(jnp.broadcast_to(on, (1, 128)), jnp.exp(last), 0.0)
        packed = packed + jnp.where(rows == q, jnp.exp(middle), 0.0)
        packed = packed + jnp.where(rows == q + 4, decay, 0.0)
        packed = packed + jnp.where(rows == q + 8, through, 0.0)
        through = through * decay
    rowp[...] = split_pack(packed)
    dmine[...] = jnp.broadcast_to(through, (8, 128))
    dline[0] = dmine[...]
    for j in range(1, LINE):
        decay_copy(j).start()

    def convolved(q, where):
        window = seqx[pl.ds(pl.multiple_of(q * BLOCK, BLOCK), BLOCK + HALO), where]
        moved = jnp.dot(shifts[q], window, preferred_element_type=F32)
        weights = 0.5 * w_ref[:, where]
        half = 0.5 * b_ref[:, where] + weights[3:4] * window[HALO:].astype(F32)
        for j in range(1, KW):
            half = half + weights[3 - j : 4 - j] * moved[(j - 1) * BLOCK : j * BLOCK]
        return (half + half * jnp.tanh(half)).astype(BF16)

    for o in range(4):
        exchange(chunks, o, tail_cols).wait_recv()
    place(tail_cols)
    halo(chunks, tail_cols).start()
    halo(chunks, tail_cols).wait_recv()

    def projections(q, carry):
        both = convolved(q, tail_cols)
        bpart = both[:, :NS]
        cpart = both[:, NS:]
        first = (me * PER_DEV + q) * BLOCK
        row_docs = docs(row + first)
        scores = lax.dot_general(cpart, bpart, (((1,), (1,)), ((), ())), preferred_element_type=F32)
        keep = (row_docs == docs(col + first)) & (col <= row)
        lhs[q, :, :BLOCK] = jnp.where(keep, scores, 0.0).astype(BF16)
        enters = row_docs == docs(first - 1)
        lhs[q, :, BLOCK:] = jnp.where(enters, cpart.astype(F32), 0.0).astype(BF16)
        stays = row_docs == docs(first + BLOCK - 1)
        btail[q] = jnp.where(stays, bpart.astype(F32), 0.0).T.astype(BF16)
        return carry

    lax.fori_loop(0, PER_DEV, projections, 0)

    for j in range(1, LINE):
        decay_copy(j).wait_recv()
    line_rows = iota((8, 128), 0)
    line_decays = jnp.zeros((8, 128), F32)
    for n in range(LINE):
        line_decays = line_decays + jnp.where(line_rows == n, dline[lax.rem(z - n + LINE, LINE)], 0.0)
    dpack[...] = split_pack(jnp.concatenate([line_decays, jnp.zeros((8, 128), F32)], axis=0))

    def stage_arrive(k):
        for o in range(4):
            exchange(k, o, cols(k)).wait_recv()
        place(cols(k))
        halo(k, cols(k)).start()

    def stage_state(k):
        where = cols(k)
        halo(k, where).wait_recv()
        rowx[k] = jnp.dot(rowp[...], spread[:, where], preferred_element_type=F32)

        def block(q, state):
            loc[q, :, where] = state
            value = convolved(q, where)
            at_rows = pl.ds(pl.multiple_of(q * BLOCK, BLOCK), BLOCK)
            mixed[at_rows, where] = value
            factor = jnp.dot(fac2[q], spread[:, where], preferred_element_type=F32)
            scaled = (value.astype(F32) * factor).astype(BF16)
            zbuf[at_rows, where] = scaled
            added = jnp.dot(btail[q], scaled, preferred_element_type=F32)
            return rowx[k, pl.ds(q + 4, 1)] * state + rowx[k, pl.ds(q, 1)] * added

        state = jnp.zeros((NS, CHUNK), F32)
        for q in range(PER_DEV):
            state = block(q, state)
        est[k] = state.astype(BF16)
        for j in range(1, LINE):
            state_copy(k, j).start()
        sbuf[k, 0] = est[k, pl.ds(pl.multiple_of(z * SLICE, SLICE), SLICE)]

    def stage_prefix(k):
        for j in range(1, LINE):
            state_copy(k, j).wait_recv()
        decays = jnp.dot(dpack[...], spread[:, cols(k)], preferred_element_type=F32)
        running = jnp.zeros((SLICE, CHUNK), F32)
        for n in range(LINE):
            runs[k, n] = running
            running = decays[n : n + 1] * running + sbuf[k, lax.rem(z - n + LINE, LINE)].astype(F32)
        lsend[k] = running
        line_copy(k).start()

    def stage_back(k):
        line_copy(k).wait_recv()
        decays = jnp.dot(dpack[...], spread[:, cols(k)], preferred_element_type=F32)
        before = jnp.where(me < LINE, 0.0, lrecv[k])
        for n in range(LINE):
            isend[k, lax.rem(n - z + LINE, LINE)] = (runs[k, n] + before).astype(BF16)
            before = before * decays[n : n + 1]
        for j in range(1, LINE):
            back_copy(k, j).start()
        inc[k, pl.ds(pl.multiple_of(z * SLICE, SLICE), SLICE)] = isend[k, 0]

    def stage_out(k):
        where = cols(k)
        for j in range(1, LINE):
            back_copy(k, j).wait_recv()
        entering = inc[k].astype(F32)
        for q in range(PER_DEV):
            at_rows = pl.ds(q * BLOCK, BLOCK)
            state = loc[q, :, where] + rowx[k, pl.ds(q + 8, 1)] * entering
            scaled = (rowx[k, pl.ds(q, 1)] * state).astype(BF16)
            right = jnp.concatenate([zbuf[at_rows, where], scaled], axis=0)
            value = jnp.dot(lhs[q], right, preferred_element_type=F32)
            factor = jnp.dot(fac1[q], spread[:, where], preferred_element_type=F32)
            skip = rowx[k, pl.ds(12, 1)] * mixed[at_rows, where].astype(F32)
            ybuf[at_rows, where] = (factor * value + skip).astype(BF16)
        write(k).start()

    def write(k):
        return pltpu.make_async_copy(ybuf.at[:, cols(k)], out_hbm.at[:, cols(k)], out_sem.at[k])

    def step(i, carry):
        @pl.when(i < chunks)
        def _():
            stage_arrive(i)

        @pl.when(i + 2 < chunks)
        def _():
            send_chunk(i + 2)

        @pl.when((i >= 1) & (i - 1 < chunks))
        def _():
            stage_state(i - 1)

        @pl.when((i >= 2) & (i - 2 < chunks))
        def _():
            stage_prefix(i - 2)

        @pl.when((i >= 3) & (i - 3 < chunks))
        def _():
            stage_back(i - 3)

        @pl.when(i >= 4)
        def _():
            stage_out(i - 4)

        return carry

    lax.fori_loop(0, chunks + 4, step, 0)

    for o in range(4):
        exchange_dt(o).wait_send()
        exchange(chunks, o, tail_cols).wait_send()
    halo(chunks, tail_cols).wait_send()
    for j in range(1, LINE):
        decay_copy(j).wait_send()

    def finish(k, carry):
        for o in range(4):
            exchange(k, o, cols(k)).wait_send()
        halo(k, cols(k)).wait_send()
        line_copy(k).wait_send()
        for j in range(1, LINE):
            state_copy(k, j).wait_send()
            back_copy(k, j).wait_send()
        write(k).wait()
        return carry

    lax.fori_loop(0, chunks, finish, 0)


def body(xbc, dt_raw, conv_weight, conv_bias, dt_bias, a_log, d_skip, doc_lengths, loader_dest):
    rows, width = xbc.shape
    heads = dt_raw.shape[1]
    inner = heads * P_SIZE
    chunks = inner // CHUNK
    devices = lax.axis_size("seq")
    params = jnp.concatenate(
        [dt_bias[None], a_log[None], d_skip[None], jnp.zeros((5, heads), F32)], axis=0)
    vmem = pl.BlockSpec(memory_space=pltpu.VMEM)
    smem = pl.BlockSpec(memory_space=pltpu.SMEM)
    anywhere = pl.BlockSpec(memory_space=pl.ANY)
    dma = pltpu.SemaphoreType.DMA
    V = pltpu.VMEM
    scratch = [
        V((PER_DEV, BLOCK, width), BF16),
        V((4, BLOCK, width), BF16),
        V((5, BLOCK, width), BF16),
        V((PER_DEV, BLOCK, heads), BF16),
        V((4, BLOCK, heads), BF16),
        V((5, BLOCK, heads), BF16),
        V((HALO + rows, width), BF16),
        V((rows, inner), BF16),
        V((rows, inner), BF16),
        V((PER_DEV, NS, inner), F32),
        V((chunks, NS, CHUNK), BF16),
        V((chunks, LINE, SLICE, CHUNK), BF16),
        V((chunks, LINE, SLICE, CHUNK), F32),
        V((chunks, SLICE, CHUNK), F32),
        V((chunks, SLICE, CHUNK), F32),
        V((chunks, LINE, SLICE, CHUNK), BF16),
        V((chunks, NS, CHUNK), BF16),
        V((rows, inner), BF16),
        V((128, inner), BF16),
        V((PER_DEV, (KW - 1) * BLOCK, BLOCK + HALO), BF16),
        V((PER_DEV, BLOCK, BLOCK + NS), BF16),
        V((PER_DEV, NS, BLOCK), BF16),
        V((PER_DEV, BLOCK, 128), BF16),
        V((PER_DEV, BLOCK, 128), BF16),
        V((16, 128), BF16),
        V((chunks, 16, CHUNK), F32),
        V((8, 128), F32),
        V((LINE, 8, 128), F32),
        V((16, 128), BF16),
        dma((chunks + 1,)), dma((1,)),
        dma((4, chunks + 1)), dma((4, chunks + 1)),
        dma((4,)), dma((4,)),
        dma((chunks + 1,)), dma((chunks + 1,)),
        dma((LINE,)), dma((LINE,)),
        dma((chunks, LINE)), dma((chunks, LINE)),
        dma((chunks,)), dma((chunks,)),
        dma((chunks, LINE)), dma((chunks, LINE)),
        dma((chunks,)),
    ]
    return pl.pallas_call(
        functools.partial(kernel, devices, heads),
        out_shape=jax.ShapeDtypeStruct((rows, inner), BF16),
        in_specs=[smem, smem, anywhere, anywhere, vmem, vmem, vmem],
        out_specs=anywhere,
        scratch_shapes=scratch,
        cost_estimate=pl.CostEstimate(flops=2_000_000_000, bytes_accessed=10_000_000, transcendentals=3_000_000),
        compiler_params=pltpu.CompilerParams(
            collective_id=0, has_side_effects=True, vmem_limit_bytes=56 * 1024 * 1024),
    )(
        doc_lengths, loader_dest,
        xbc.reshape(PER_DEV, BLOCK, width), dt_raw.reshape(PER_DEV, BLOCK, heads),
        conv_weight, conv_bias.reshape(1, width), params,
    )


def solution(mesh):
    placed = (
        P(("dp", "seq"), None),
        P(("dp", "seq"), None),
        P(),
        P(),
        P(),
        P(),
        P(),
        P("dp"),
        P("dp"),
    )
    return jax.shard_map(
        body, mesh=mesh, in_specs=placed, out_specs=P(("dp", "seq"), None), check_vma=False
    )
```

time: 984 us -> 156 us (0.16)
  the two profiles are of different devices: /device:TPU:1 before, /device:TPU:8 now
where the time goes in v1:
time: 156 us; the launch traced here: 155 us
  Pallas kernels  146 us (94%)
  local copies, waits for them, and re-layouts  7.71 us (5%)
    pallas_call x1, Pallas kernels, body(): pl.pallas_call(functools.partial(kernel, devices, heads), out_shape=jax.S...  146 us
    unnamed x2, local copies, waits for them, and re-layouts  6.3 us

profile of v1, /device:TPU:8, one launch (start us, length us, event | category | flops | bytes accessed | tf_op | source)
XLA Modules:
  0.0 155.3 jit_solution(12730032622031434241)
XLA Ops:
  0.0 0.1 pad.3.clone
  0.1 1.3 maximum_maximum_fusion.par_ref
  1.4 1.3 reshape.11.b_ref
  2.8 1.6 %copy.10 = bf16[512,64]{1,0:T(8,128)(2,1)} copy(bf16[512,64]{0,1:T(8,128)(2,1)} %param.10) | data formatting | bytes 131072 | tf_op args[1]
  4.4 146.2 %shard_map.91 = bf16[512,4096]{1,0:T(8,128)(2,1)} custom-call(s32[16]{0:T(128)} %lens.1, s32[128]{0:T(128)} %dest.1, bf16[4,128,4352]{2,1,0:T(8,128)(2,1)} %bitcast.5, bf16[4,128,64]{2,1,0:T(8,128)(2,1)} %bitcast.6, f32[4,4352]{1,0:T(4,128)} %w_ref.1, f32[1,4352]{1,0:T(1,128)} %reshape.11.b_ref, f32[8,64]{1,0:T(8,128)} %maximum_maximum_fusion.par_ref), custom_call_target="tpu_custom_call" | custom-call | flops 2000000000 | bytes 10000000 | tf_op jit(solution)/shard_map/pallas_call | solution.py:457
  150.6 4.7 %copy.12 = bf16[512,4096]{1,0:T(8,128)(2,1)} copy(bf16[512,4096]{1,0:T(8,128)(2,1)} %shard_map.91) | data formatting | bytes 8388608
  (1 shorter events, 0.0 us)

commit v2 on v1

--- a/solution.py
+++ b/solution.py
@@ -15,6 +15,8 @@
 LINE = 8
 HALO = 16
 CHUNK = 512
+AHEAD = 2
+LAGS = (1, 3, 6, 9)
 OFFSETS = (-2, -1, 1, 2)
 SLICE = NS // LINE
 MESH = pl.DeviceIdType.MESH
@@ -40,7 +42,7 @@
 
 def kernel(
     devices, heads,
-    lens, dest, x_hbm, dt_hbm, w_ref, b_ref, par_ref,
+    lens, dest, x_hbm, dt_hbm, w_ref, b_ref, dtb_ref, alog_ref, skip_ref,
     out_hbm,
     xin, send, recv, dtin, dtsend, dtrecv, seqx, mixed, zbuf, loc, est, sbuf, runs,
     lsend, lrecv, isend, inc, ybuf, spread, shifts, lhs, btail, fac1, fac2, rowp, rowx,
@@ -160,7 +162,7 @@
             exchange(k, o, cols(k)).start()
 
     load_dt.wait()
-    dt_blocks = [dtin[j] for j in range(PER_DEV)]
+    dt_blocks = [dtin[:, j * BLOCK : (j + 1) * BLOCK] for j in range(PER_DEV)]
     for o, offset in enumerate(OFFSETS):
         dtsend[o] = chosen(picks[offset + 2], dt_blocks)
     dtrecv[4] = chosen(picks[2], dt_blocks)
@@ -170,8 +172,8 @@
     for o in range(4):
         exchange_dt(o).start()
         exchange(chunks, o, tail_cols).start()
-    send_chunk(0)
-    send_chunk(1)
+    for k in range(AHEAD):
+        send_chunk(k)
 
     starts = []
     total = jnp.int32(0)
@@ -191,7 +193,7 @@
 
     def make_shift(q, carry):
         first = (me * PER_DEV + q) * BLOCK
-        same = docs(iota(square, 0) + first) == docs(iota(square, 1) + (first - HALO))
+        same = docs(iota((BLOCK, 1), 0) + first) == docs(iota((1, BLOCK + HALO), 1) + (first - HALO))
         apart = iota(square, 1) - iota(square, 0)
         for j in range(1, KW):
             keep = same & (apart == HALO - j)
@@ -209,7 +211,9 @@
     lax.fori_loop(0, chunks, make_spread, 0)
 
     double = jnp.where((iota((heads, 128), 1) & 63) == iota((heads, 128), 0), 1.0, 0.0)
-    params = jnp.dot(par_ref[...], double, precision=lax.Precision.HIGHEST, preferred_element_type=F32)
+    which = iota((8, heads), 0)
+    stacked = jnp.where(which == 0, dtb_ref[...], jnp.where(which == 1, alog_ref[...], skip_ref[...]))
+    params = jnp.dot(stacked, double, precision=lax.Precision.HIGHEST, preferred_element_type=F32)
     lower = jnp.where(col <= row, 1.0, 0.0)
 
     for o in range(4):
@@ -219,7 +223,9 @@
     rows = iota((16, 128), 0)
     packed = jnp.where(rows == 12, params[2:3], 0.0)
     for q in range(PER_DEV):
-        raw = jnp.dot(chosen(origin[q], dt_options), double.astype(BF16), preferred_element_type=F32) + params[0:1]
+        raw = lax.dot_general(
+            chosen(origin[q], dt_options), double.astype(BF16), (((0,), (0,)), ((), ())),
+            preferred_element_type=F32) + params[0:1]
         dt = jnp.maximum(raw, 0.0) + jnp.log1p(jnp.exp(-jnp.abs(raw)))
         rate = -jnp.exp(params[1:2]) * dt
         cum = jnp.dot(lower, rate, precision=lax.Precision.HIGHEST, preferred_element_type=F32)
@@ -244,7 +250,7 @@
         window = seqx[pl.ds(pl.multiple_of(q * BLOCK, BLOCK), BLOCK + HALO), where]
         moved = jnp.dot(shifts[q], window, preferred_element_type=F32)
         weights = 0.5 * w_ref[:, where]
-        half = 0.5 * b_ref[:, where] + weights[3:4] * window[HALO:].astype(F32)
+        half = 0.5 * b_ref[where].reshape(1, -1) + weights[3:4] * window[HALO:].astype(F32)
         for j in range(1, KW):
             half = half + weights[3 - j : 4 - j] * moved[(j - 1) * BLOCK : j * BLOCK]
         return (half + half * jnp.tanh(half)).astype(BF16)
@@ -253,16 +259,15 @@
         exchange(chunks, o, tail_cols).wait_recv()
     place(tail_cols)
     halo(chunks, tail_cols).start()
-    halo(chunks, tail_cols).wait_recv()
 
     def projections(q, carry):
         both = convolved(q, tail_cols)
         bpart = both[:, :NS]
         cpart = both[:, NS:]
         first = (me * PER_DEV + q) * BLOCK
-        row_docs = docs(row + first)
+        row_docs = docs(iota((BLOCK, 1), 0) + first)
         scores = lax.dot_general(cpart, bpart, (((1,), (1,)), ((), ())), preferred_element_type=F32)
-        keep = (row_docs == docs(col + first)) & (col <= row)
+        keep = (row_docs == docs(iota((1, BLOCK), 1) + first)) & (col <= row)
         lhs[q, :, :BLOCK] = jnp.where(keep, scores, 0.0).astype(BF16)
         enters = row_docs == docs(first - 1)
         lhs[q, :, BLOCK:] = jnp.where(enters, cpart.astype(F32), 0.0).astype(BF16)
@@ -270,15 +275,18 @@
         btail[q] = jnp.where(stays, bpart.astype(F32), 0.0).T.astype(BF16)
         return carry
 
-    lax.fori_loop(0, PER_DEV, projections, 0)
-
-    for j in range(1, LINE):
-        decay_copy(j).wait_recv()
-    line_rows = iota((8, 128), 0)
-    line_decays = jnp.zeros((8, 128), F32)
-    for n in range(LINE):
-        line_decays = line_decays + jnp.where(line_rows == n, dline[lax.rem(z - n + LINE, LINE)], 0.0)
-    dpack[...] = split_pack(jnp.concatenate([line_decays, jnp.zeros((8, 128), F32)], axis=0))
+    def prepare_projections():
+        halo(chunks, tail_cols).wait_recv()
+        lax.fori_loop(0, PER_DEV, projections, 0)
+
+    def prepare_decays():
+        for j in range(1, LINE):
+            decay_copy(j).wait_recv()
+        line_rows = iota((8, 128), 0)
+        line_decays = jnp.zeros((8, 128), F32)
+        for n in range(LINE):
+            line_decays = line_decays + jnp.where(line_rows == n, dline[lax.rem(z - n + LINE, LINE)], 0.0)
+        dpack[...] = split_pack(jnp.concatenate([line_decays, jnp.zeros((8, 128), F32)], axis=0))
 
     def stage_arrive(k):
         for o in range(4):
@@ -356,29 +364,33 @@
         def _():
             stage_arrive(i)
 
-        @pl.when(i + 2 < chunks)
-        def _():
-            send_chunk(i + 2)
-
-        @pl.when((i >= 1) & (i - 1 < chunks))
-        def _():
-            stage_state(i - 1)
-
-        @pl.when((i >= 2) & (i - 2 < chunks))
-        def _():
-            stage_prefix(i - 2)
-
-        @pl.when((i >= 3) & (i - 3 < chunks))
-        def _():
-            stage_back(i - 3)
-
-        @pl.when(i >= 4)
-        def _():
-            stage_out(i - 4)
-
-        return carry
-
-    lax.fori_loop(0, chunks + 4, step, 0)
+        pl.when(i == LAGS[0])(prepare_projections)
+
+        @pl.when((i >= LAGS[0]) & (i - LAGS[0] < chunks))
+        def _():
+            stage_state(i - LAGS[0])
+
+        pl.when(i == LAGS[1])(prepare_decays)
+
+        @pl.when((i >= LAGS[1]) & (i - LAGS[1] < chunks))
+        def _():
+            stage_prefix(i - LAGS[1])
+
+        @pl.when((i >= LAGS[2]) & (i - LAGS[2] < chunks))
+        def _():
+            stage_back(i - LAGS[2])
+
+        @pl.when(i + AHEAD < chunks)
+        def _():
+            send_chunk(i + AHEAD)
+
+        @pl.when((i >= LAGS[3]) & (i - LAGS[3] < chunks))
+        def _():
+            stage_out(i - LAGS[3])
+
+        return carry
+
+    lax.fori_loop(0, chunks + LAGS[-1], step, 0)
 
     for o in range(4):
         exchange_dt(o).wait_send()
@@ -407,8 +419,6 @@
     inner = heads * P_SIZE
     chunks = inner // CHUNK
     devices = lax.axis_size("seq")
-    params = jnp.concatenate(
-        [dt_bias[None], a_log[None], d_skip[None], jnp.zeros((5, heads), F32)], axis=0)
     vmem = pl.BlockSpec(memory_space=pltpu.VMEM)
     smem = pl.BlockSpec(memory_space=pltpu.SMEM)
     anywhere = pl.BlockSpec(memory_space=pl.ANY)
@@ -418,9 +428,9 @@
         V((PER_DEV, BLOCK, width), BF16),
         V((4, BLOCK, width), BF16),
         V((5, BLOCK, width), BF16),
-        V((PER_DEV, BLOCK, heads), BF16),
-        V((4, BLOCK, heads), BF16),
-        V((5, BLOCK, heads), BF16),
+        V((heads, rows), BF16),
+        V((4, heads, BLOCK), BF16),
+        V((5, heads, BLOCK), BF16),
         V((HALO + rows, width), BF16),
         V((rows, inner), BF16),
         V((rows, inner), BF16),
@@ -457,16 +467,16 @@
     return pl.pallas_call(
         functools.partial(kernel, devices, heads),
         out_shape=jax.ShapeDtypeStruct((rows, inner), BF16),
-        in_specs=[smem, smem, anywhere, anywhere, vmem, vmem, vmem],
+        in_specs=[smem, smem, anywhere, anywhere, vmem, vmem, vmem, vmem, vmem],
         out_specs=anywhere,
         scratch_shapes=scratch,
         cost_estimate=pl.CostEstimate(flops=2_000_000_000, bytes_accessed=10_000_000, transcendentals=3_000_000),
         compiler_params=pltpu.CompilerParams(
-            collective_id=0, has_side_effects=True, vmem_limit_bytes=56 * 1024 * 1024),
+            collective_id=0, has_side_effects=True, vmem_limit_bytes=63 * 1024 * 1024),
     )(
         doc_lengths, loader_dest,
-        xbc.reshape(PER_DEV, BLOCK, width), dt_raw.reshape(PER_DEV, BLOCK, heads),
-        conv_weight, conv_bias.reshape(1, width), params,
+        xbc.reshape(PER_DEV, BLOCK, width), dt_raw.T,
+        conv_weight, conv_bias, dt_bias[None], a_log[None], d_skip[None],
     )
 
 

time: 156 us -> 142 us (0.910)
  the two profiles are of different devices: /device:TPU:8 before, /device:TPU:1 now
where the time goes in v2:
time: 142 us; the launch traced here: 140 us
  Pallas kernels  136 us (96%)
  local copies, waits for them, and re-layouts  4.7 us (3%)
    pallas_call x1, Pallas kernels, body(): pl.pallas_call(functools.partial(kernel, devices, heads), out_shape=jax.S...  136 us
    unnamed x1, local copies, waits for them, and re-layouts  4.7 us

profile of v2, /device:TPU:1, one launch (start us, length us, event | category | flops | bytes accessed | tf_op | source)
XLA Modules:
  0.0 140.3 jit_solution(17176832841327005756)
XLA Ops:
  0.0 135.5 %shard_map.91 = bf16[512,4096]{1,0:T(8,128)(2,1)} custom-call(s32[16]{0:T(128)} %lens.1, s32[128]{0:T(128)} %dest.1, bf16[4,128,4352]{2,1,0:T(8,128)(2,1)} %bitcast.5, bf16[64,512]{1,0:T(8,128)(2,1)} %bitcast.6, f32[4,4352]{1,0:T(4,128)} %w_ref.1, f32[4352]{0:T(1024)} %b_ref.1, f32[1,64]{1,0:T(1,128)} %bitcast.7, f32[1,64]{1,0:T(1,128)} %bitcast.8, ...), custom_call_target="tpu_custom_call" | custom-call | flops 2000000000 | bytes 10000000 | tf_op jit(solution)/shard_map/pallas_call | solution.py:467
  135.6 4.7 %copy.11 = bf16[512,4096]{1,0:T(8,128)(2,1)} copy(bf16[512,4096]{1,0:T(8,128)(2,1)} %shard_map.91) | data formatting | bytes 8388608

commit v3 on v2

--- a/solution.py
+++ b/solution.py
@@ -16,9 +16,10 @@
 HALO = 16
 CHUNK = 512
 AHEAD = 2
-LAGS = (1, 3, 6, 9)
+LAGS = (1, 2, 4, 6, 8, 10)
 OFFSETS = (-2, -1, 1, 2)
 SLICE = NS // LINE
+PAIRS = LINE // 2
 MESH = pl.DeviceIdType.MESH
 F32 = jnp.float32
 BF16 = jnp.bfloat16
@@ -44,20 +45,25 @@
     devices, heads,
     lens, dest, x_hbm, dt_hbm, w_ref, b_ref, dtb_ref, alog_ref, skip_ref,
     out_hbm,
-    xin, send, recv, dtin, dtsend, dtrecv, seqx, mixed, zbuf, loc, est, sbuf, runs,
-    lsend, lrecv, isend, inc, ybuf, spread, shifts, lhs, btail, fac1, fac2, rowp, rowx,
-    dmine, dline, dpack,
+    xin, send, recv, dtin, dtsend, dtrecv, seqx, mixed, zbuf, loc, est, est32, sin, sbuf, runs,
+    lsend, lrecv, isend, rsend, inc, ybuf, spread, shifts, lhs, btail, fac1, fac2, rowp, rowx,
+    dmine, dline, dpack, decx,
     in_sem, dt_sem, x_send, x_recv, d_send, d_recv, h_send, h_recv, t_send, t_recv,
-    s_send, s_recv, l_send, l_recv, i_send, i_recv, out_sem,
+    s_send, s_recv, l_send, l_recv, i_send, i_recv, p_send, p_recv, r_send, r_recv, out_sem,
 ):
     inner = heads * P_SIZE
     chunks = inner // CHUNK
     me = lax.axis_index("seq")
-    z = lax.rem(me, LINE)
-    base = me - z
+    z = lax.rem(me - lax.rem(lax.axis_index("dp"), 2) + devices, LINE)
+    pair = lax.shift_right_logical(z, 1)
+    even = lax.rem(z, 2) == 0
+    odd = lax.rem(z, 2) == 1
 
     def at(offset):
         return lax.rem(me + offset + devices, devices)
+
+    def member(place):
+        return at(place - z)
 
     def cols(k):
         return pl.ds(pl.multiple_of(k * CHUNK, CHUNK), CHUNK)
@@ -79,7 +85,7 @@
     lax.fori_loop(0, chunks, start_load, 0)
 
     barrier = pltpu.get_barrier_semaphore()
-    partners = [at(o) for o in OFFSETS] + [base + lax.rem(z + j, LINE) for j in range(1, LINE)] + [at(LINE), at(-LINE)]
+    partners = [at(o) for o in OFFSETS] + [member(lax.rem(z + j, LINE)) for j in range(1, LINE)] + [at(LINE), at(-LINE)]
     for partner in partners:
         pl.semaphore_signal(barrier, inc=1, device_id={"seq": partner}, device_id_type=MESH)
 
@@ -122,14 +128,26 @@
         return pltpu.make_async_remote_copy(
             src_ref=dmine, dst_ref=dline.at[j],
             send_sem=t_send.at[j], recv_sem=t_recv.at[j],
-            device_id={"seq": base + lax.rem(z + j, LINE)}, device_id_type=MESH)
-
-    def state_copy(k, j):
+            device_id={"seq": member(lax.rem(z + j, LINE))}, device_id_type=MESH)
+
+    def pair_copy(k):
+        return pltpu.make_async_remote_copy(
+            src_ref=est.at[k], dst_ref=sin.at[k],
+            send_sem=p_send.at[k], recv_sem=p_recv.at[k],
+            device_id={"seq": at(-1)}, device_id_type=MESH)
+
+    def relay_copy(k):
+        return pltpu.make_async_remote_copy(
+            src_ref=rsend.at[k], dst_ref=inc.at[k],
+            send_sem=r_send.at[k], recv_sem=r_recv.at[k],
+            device_id={"seq": at(1)}, device_id_type=MESH)
+
+    def state_copy(k, j, sender):
         target = lax.rem(z + j, LINE)
         return pltpu.make_async_remote_copy(
-            src_ref=est.at[k, pl.ds(pl.multiple_of(target * SLICE, SLICE), SLICE)], dst_ref=sbuf.at[k, j],
-            send_sem=s_send.at[k, j], recv_sem=s_recv.at[k, j],
-            device_id={"seq": base + target}, device_id_type=MESH)
+            src_ref=est.at[k, pl.ds(pl.multiple_of(target * SLICE, SLICE), SLICE)], dst_ref=sbuf.at[k, sender],
+            send_sem=s_send.at[k, j], recv_sem=s_recv.at[k, sender],
+            device_id={"seq": member(target)}, device_id_type=MESH)
 
     def line_copy(k):
         return pltpu.make_async_remote_copy(
@@ -137,12 +155,11 @@
             send_sem=l_send.at[k], recv_sem=l_recv.at[k],
             device_id={"seq": at(LINE)}, device_id_type=MESH)
 
-    def back_copy(k, j):
-        target = lax.rem(z + j, LINE)
-        return pltpu.make_async_remote_copy(
-            src_ref=isend.at[k, j], dst_ref=inc.at[k, pl.ds(pl.multiple_of(z * SLICE, SLICE), SLICE)],
-            send_sem=i_send.at[k, j], recv_sem=i_recv.at[k, j],
-            device_id={"seq": base + target}, device_id_type=MESH)
+    def back_copy(k, p, sender):
+        return pltpu.make_async_remote_copy(
+            src_ref=isend.at[k, p], dst_ref=inc.at[k, pl.ds(pl.multiple_of(sender * SLICE, SLICE), SLICE)],
+            send_sem=i_send.at[k, p], recv_sem=i_recv.at[k, sender],
+            device_id={"seq": member(2 * p)}, device_id_type=MESH)
 
     def fill(where):
         blocks = [xin[j, :, where] for j in range(PER_DEV)]
@@ -313,37 +330,70 @@
         state = jnp.zeros((NS, CHUNK), F32)
         for q in range(PER_DEV):
             state = block(q, state)
-        est[k] = state.astype(BF16)
-        for j in range(1, LINE):
-            state_copy(k, j).start()
-        sbuf[k, 0] = est[k, pl.ds(pl.multiple_of(z * SLICE, SLICE), SLICE)]
+        est32[k] = state
+
+        @pl.when(odd)
+        def _():
+            est[k] = state.astype(BF16)
+            pair_copy(k).start()
+
+    def stage_pair(k):
+        decx[k] = jnp.dot(dpack[...], spread[:, cols(k)], preferred_element_type=F32)
+
+        @pl.when(even)
+        def _():
+            pair_copy(k).wait_recv()
+            est[k] = (decx[k, pl.ds(z + 1, 1)] * est32[k] + sin[k].astype(F32)).astype(BF16)
+            for j in range(1, LINE):
+                state_copy(k, j, pair).start()
+            sbuf[k, pair] = est[k, pl.ds(pl.multiple_of(z * SLICE, SLICE), SLICE)]
 
     def stage_prefix(k):
-        for j in range(1, LINE):
-            state_copy(k, j).wait_recv()
-        decays = jnp.dot(dpack[...], spread[:, cols(k)], preferred_element_type=F32)
+        for p in range(PAIRS):
+            @pl.when(z != 2 * p)
+            def _(p=p):
+                state_copy(k, 1, p).wait_recv()
+        decays = decx[k]
         running = jnp.zeros((SLICE, CHUNK), F32)
-        for n in range(LINE):
-            runs[k, n] = running
-            running = decays[n : n + 1] * running + sbuf[k, lax.rem(z - n + LINE, LINE)].astype(F32)
+        for p in range(PAIRS):
+            runs[k, p] = running
+            both = decays[2 * p : 2 * p + 1] * decays[2 * p + 1 : 2 * p + 2]
+            running = both * running + sbuf[k, p].astype(F32)
         lsend[k] = running
         line_copy(k).start()
 
     def stage_back(k):
         line_copy(k).wait_recv()
-        decays = jnp.dot(dpack[...], spread[:, cols(k)], preferred_element_type=F32)
-        before = jnp.where(me < LINE, 0.0, lrecv[k])
-        for n in range(LINE):
-            isend[k, lax.rem(n - z + LINE, LINE)] = (runs[k, n] + before).astype(BF16)
-            before = before * decays[n : n + 1]
-        for j in range(1, LINE):
-            back_copy(k, j).start()
-        inc[k, pl.ds(pl.multiple_of(z * SLICE, SLICE), SLICE)] = isend[k, 0]
+        decays = decx[k]
+        before = lrecv[k]
+        for p in range(PAIRS):
+            isend[k, p] = (runs[k, p] + before).astype(BF16)
+            before = before * (decays[2 * p : 2 * p + 1] * decays[2 * p + 1 : 2 * p + 2])
+        for p in range(PAIRS):
+            @pl.when(z != 2 * p)
+            def _(p=p):
+                back_copy(k, p, z).start()
+
+        @pl.when(even)
+        def _():
+            inc[k, pl.ds(pl.multiple_of(z * SLICE, SLICE), SLICE)] = isend[k, pair]
+
+    def stage_relay(k):
+        @pl.when(even)
+        def _():
+            for owner in range(LINE):
+                @pl.when(z != owner)
+                def _(owner=owner):
+                    back_copy(k, 0, owner).wait_recv()
+            rsend[k] = (decx[k, pl.ds(z, 1)] * inc[k].astype(F32) + est32[k]).astype(BF16)
+            relay_copy(k).start()
 
     def stage_out(k):
         where = cols(k)
-        for j in range(1, LINE):
-            back_copy(k, j).wait_recv()
+        @pl.when(odd)
+        def _():
+            relay_copy(k).wait_recv()
+
         entering = inc[k].astype(F32)
         for q in range(PER_DEV):
             at_rows = pl.ds(q * BLOCK, BLOCK)
@@ -374,19 +424,27 @@
 
         @pl.when((i >= LAGS[1]) & (i - LAGS[1] < chunks))
         def _():
-            stage_prefix(i - LAGS[1])
+            stage_pair(i - LAGS[1])
 
         @pl.when((i >= LAGS[2]) & (i - LAGS[2] < chunks))
         def _():
-            stage_back(i - LAGS[2])
+            stage_prefix(i - LAGS[2])
+
+        @pl.when((i >= LAGS[3]) & (i - LAGS[3] < chunks))
+        def _():
+            stage_back(i - LAGS[3])
+
+        @pl.when((i >= LAGS[4]) & (i - LAGS[4] < chunks))
+        def _():
+            stage_relay(i - LAGS[4])
 
         @pl.when(i + AHEAD < chunks)
         def _():
             send_chunk(i + AHEAD)
 
-        @pl.when((i >= LAGS[3]) & (i - LAGS[3] < chunks))
-        def _():
-            stage_out(i - LAGS[3])
+        @pl.when((i >= LAGS[5]) & (i - LAGS[5] < chunks))
+        def _():
+            stage_out(i - LAGS[5])
 
         return carry
 
@@ -404,13 +462,39 @@
             exchange(k, o, cols(k)).wait_send()
         halo(k, cols(k)).wait_send()
         line_copy(k).wait_send()
-        for j in range(1, LINE):
-            state_copy(k, j).wait_send()
-            back_copy(k, j).wait_send()
+        for p in range(PAIRS):
+            @pl.when(z != 2 * p)
+            def _(p=p):
+                back_copy(k, p, z).wait_send()
+
+        @pl.when(even)
+        def _():
+            for j in range(1, LINE):
+                state_copy(k, j, pair).wait_send()
+            relay_copy(k).wait_send()
+
+        @pl.when(odd)
+        def _():
+            pair_copy(k).wait_send()
+
         write(k).wait()
         return carry
 
     lax.fori_loop(0, chunks, finish, 0)
+
+
+def hand_over(source, target, held, in_sem, out_sem):
+    rows = source.shape[0] // PER_DEV
+    parts = [pl.ds(n * rows, rows) for n in range(PER_DEV)]
+    reads = [pltpu.make_async_copy(source.at[part], held.at[part], in_sem.at[n]) for n, part in enumerate(parts)]
+    writes = [pltpu.make_async_copy(held.at[part], target.at[part], out_sem.at[n]) for n, part in enumerate(parts)]
+    for read in reads:
+        read.start()
+    for read, write in zip(reads, writes):
+        read.wait()
+        write.start()
+    for write in writes:
+        write.wait()
 
 
 def body(xbc, dt_raw, conv_weight, conv_bias, dt_bias, a_log, d_skip, doc_lengths, loader_dest):
@@ -436,11 +520,14 @@
         V((rows, inner), BF16),
         V((PER_DEV, NS, inner), F32),
         V((chunks, NS, CHUNK), BF16),
-        V((chunks, LINE, SLICE, CHUNK), BF16),
-        V((chunks, LINE, SLICE, CHUNK), F32),
+        V((chunks, NS, CHUNK), F32),
+        V((chunks, NS, CHUNK), BF16),
+        V((chunks, PAIRS, SLICE, CHUNK), BF16),
+        V((chunks, PAIRS, SLICE, CHUNK), F32),
         V((chunks, SLICE, CHUNK), F32),
         V((chunks, SLICE, CHUNK), F32),
-        V((chunks, LINE, SLICE, CHUNK), BF16),
+        V((chunks, PAIRS, SLICE, CHUNK), BF16),
+        V((chunks, NS, CHUNK), BF16),
         V((chunks, NS, CHUNK), BF16),
         V((rows, inner), BF16),
         V((128, inner), BF16),
@@ -454,17 +541,20 @@
         V((8, 128), F32),
         V((LINE, 8, 128), F32),
         V((16, 128), BF16),
+        V((chunks, 16, CHUNK), F32),
         dma((chunks + 1,)), dma((1,)),
         dma((4, chunks + 1)), dma((4, chunks + 1)),
         dma((4,)), dma((4,)),
         dma((chunks + 1,)), dma((chunks + 1,)),
         dma((LINE,)), dma((LINE,)),
-        dma((chunks, LINE)), dma((chunks, LINE)),
+        dma((chunks, LINE)), dma((chunks, PAIRS)),
         dma((chunks,)), dma((chunks,)),
-        dma((chunks, LINE)), dma((chunks, LINE)),
+        dma((chunks, PAIRS)), dma((chunks, LINE)),
+        dma((chunks,)), dma((chunks,)),
+        dma((chunks,)), dma((chunks,)),
         dma((chunks,)),
     ]
-    return pl.pallas_call(
+    result = pl.pallas_call(
         functools.partial(kernel, devices, heads),
         out_shape=jax.ShapeDtypeStruct((rows, inner), BF16),
         in_specs=[smem, smem, anywhere, anywhere, vmem, vmem, vmem, vmem, vmem],
@@ -478,6 +568,14 @@
         xbc.reshape(PER_DEV, BLOCK, width), dt_raw.T,
         conv_weight, conv_bias, dt_bias[None], a_log[None], d_skip[None],
     )
+    return pl.pallas_call(
+        hand_over,
+        out_shape=jax.ShapeDtypeStruct((rows, inner), BF16),
+        in_specs=[anywhere],
+        out_specs=anywhere,
+        scratch_shapes=[V((rows, inner), BF16), dma((PER_DEV,)), dma((PER_DEV,))],
+        compiler_params=pltpu.CompilerParams(vmem_limit_bytes=62 * 1024 * 1024),
+    )(result)
 
 
 def solution(mesh):

time: 142 us -> 140 us (0.986); the launches traced: 140 us -> 140 us
  local copies, waits for them, and re-layouts: 4.7 us -> 0 us
  Pallas kernels: 136 us -> 140 us
    unnamed x1 -> x0, local copies, waits for them, and re-layouts: 4.7 us -> none
    pallas_call x0 -> x1, Pallas kernels: none -> 3.3 us  [body(): pl.pallas_call(hand_over, out_shape=jax.ShapeDtypeStruct((rows, inner), B...]
where the time goes in v3:
time: 140 us
  Pallas kernels  140 us (100%)
    pallas_call x1, Pallas kernels, body(): pl.pallas_call(functools.partial(kernel, devices, heads), out_shape=jax.S...  137 us
    pallas_call x1, Pallas kernels, body(): pl.pallas_call(hand_over, out_shape=jax.ShapeDtypeStruct((rows, inner), B...  3.3 us

profile of v3, /device:TPU:1, one launch (start us, length us, event | category | flops | bytes accessed | tf_op | source)
XLA Modules:
  0.0 140.0 jit_solution(3052384166063125126)
XLA Ops:
  0.0 136.7 %shard_map.91.source = bf16[512,4096]{1,0:T(8,128)(2,1)} custom-call(s32[16]{0:T(128)} %lens.1, s32[128]{0:T(128)} %dest.1, bf16[4,128,4352]{2,1,0:T(8,128)(2,1)} %bitcast.5, bf16[64,512]{1,0:T(8,128)(2,1)} %bitcast.6, f32[4,4352]{1,0:T(4,128)} %w_ref.1, f32[4352]{0:T(1024)} %b_ref.1, f32[1,64]{1,0:T(1,128)} %bitcast.7, f32[1,64]{1,0:T(1,128)} %bitcast.8, ...), custom_call_target="tpu_custom_call" | custom-call | flops 2000000000 | bytes 10000000 | tf_op jit(solution)/shard_map/pallas_call | solution.py:557
  136.7 3.3 %shard_map.92 = bf16[512,4096]{1,0:T(8,128)(2,1)} custom-call(bf16[512,4096]{1,0:T(8,128)(2,1)} %shard_map.91.source), custom_call_target="tpu_custom_call" | custom-call | tf_op jit(solution)/shard_map/pallas_call | solution.py:571

commit v4 on v3

--- a/solution.py
+++ b/solution.py
@@ -18,8 +18,8 @@
 AHEAD = 2
 LAGS = (1, 2, 4, 6, 8, 10)
 OFFSETS = (-2, -1, 1, 2)
-SLICE = NS // LINE
 PAIRS = LINE // 2
+SLICE = NS // PAIRS
 MESH = pl.DeviceIdType.MESH
 F32 = jnp.float32
 BF16 = jnp.bfloat16
@@ -143,11 +143,11 @@
             device_id={"seq": at(1)}, device_id_type=MESH)
 
     def state_copy(k, j, sender):
-        target = lax.rem(z + j, LINE)
+        target = lax.rem(pair + j, PAIRS)
         return pltpu.make_async_remote_copy(
             src_ref=est.at[k, pl.ds(pl.multiple_of(target * SLICE, SLICE), SLICE)], dst_ref=sbuf.at[k, sender],
             send_sem=s_send.at[k, j], recv_sem=s_recv.at[k, sender],
-            device_id={"seq": member(target)}, device_id_type=MESH)
+            device_id={"seq": member(2 * target)}, device_id_type=MESH)
 
     def line_copy(k):
         return pltpu.make_async_remote_copy(
@@ -344,13 +344,13 @@
         def _():
             pair_copy(k).wait_recv()
             est[k] = (decx[k, pl.ds(z + 1, 1)] * est32[k] + sin[k].astype(F32)).astype(BF16)
-            for j in range(1, LINE):
+            for j in range(1, PAIRS):
                 state_copy(k, j, pair).start()
-            sbuf[k, pair] = est[k, pl.ds(pl.multiple_of(z * SLICE, SLICE), SLICE)]
+            sbuf[k, pair] = est[k, pl.ds(pl.multiple_of(pair * SLICE, SLICE), SLICE)]
 
     def stage_prefix(k):
         for p in range(PAIRS):
-            @pl.when(z != 2 * p)
+            @pl.when(pair != p)
             def _(p=p):
                 state_copy(k, 1, p).wait_recv()
         decays = decx[k]
@@ -370,19 +370,17 @@
             isend[k, p] = (runs[k, p] + before).astype(BF16)
             before = before * (decays[2 * p : 2 * p + 1] * decays[2 * p + 1 : 2 * p + 2])
         for p in range(PAIRS):
-            @pl.when(z != 2 * p)
+            @pl.when(pair != p)
             def _(p=p):
-                back_copy(k, p, z).start()
-
-        @pl.when(even)
-        def _():
-            inc[k, pl.ds(pl.multiple_of(z * SLICE, SLICE), SLICE)] = isend[k, pair]
+                back_copy(k, p, pair).start()
+
+        inc[k, pl.ds(pl.multiple_of(pair * SLICE, SLICE), SLICE)] = isend[k, pair]
 
     def stage_relay(k):
         @pl.when(even)
         def _():
-            for owner in range(LINE):
-                @pl.when(z != owner)
+            for owner in range(PAIRS):
+                @pl.when(pair != owner)
                 def _(owner=owner):
                     back_copy(k, 0, owner).wait_recv()
             rsend[k] = (decx[k, pl.ds(z, 1)] * inc[k].astype(F32) + est32[k]).astype(BF16)
@@ -426,11 +424,11 @@
         def _():
             stage_pair(i - LAGS[1])
 
-        @pl.when((i >= LAGS[2]) & (i - LAGS[2] < chunks))
+        @pl.when(even & (i >= LAGS[2]) & (i - LAGS[2] < chunks))
         def _():
             stage_prefix(i - LAGS[2])
 
-        @pl.when((i >= LAGS[3]) & (i - LAGS[3] < chunks))
+        @pl.when(even & (i >= LAGS[3]) & (i - LAGS[3] < chunks))
         def _():
             stage_back(i - LAGS[3])
 
@@ -461,17 +459,17 @@
         for o in range(4):
             exchange(k, o, cols(k)).wait_send()
         halo(k, cols(k)).wait_send()
-        line_copy(k).wait_send()
         for p in range(PAIRS):
-            @pl.when(z != 2 * p)
+            @pl.when(even & (pair != p))
             def _(p=p):
-                back_copy(k, p, z).wait_send()
+                back_copy(k, p, pair).wait_send()
 
         @pl.when(even)
         def _():
-            for j in range(1, LINE):
+            for j in range(1, PAIRS):
                 state_copy(k, j, pair).wait_send()
             relay_copy(k).wait_send()
+            line_copy(k).wait_send()
 
         @pl.when(odd)
         def _():

time: 140 us -> 142 us (1.014)
  Pallas kernels: 140 us -> 142 us
    pallas_call x1, Pallas kernels: 137 us -> 138 us  [body(): pl.pallas_call(functools.partial(kernel, devices, heads), out_shape=jax.S...]
where the time goes in v4:
time: 142 us
  Pallas kernels  142 us (100%)
    pallas_call x1, Pallas kernels, body(): pl.pallas_call(functools.partial(kernel, devices, heads), out_shape=jax.S...  138 us
    pallas_call x1, Pallas kernels, body(): pl.pallas_call(hand_over, out_shape=jax.ShapeDtypeStruct((rows, inner), B...  3.3 us

profile of v4, /device:TPU:1, one launch (start us, length us, event | category | flops | bytes accessed | tf_op | source)
XLA Modules:
  0.0 141.8 jit_solution(6153815256810277594)
XLA Ops:
  0.0 138.5 %shard_map.91.source = bf16[512,4096]{1,0:T(8,128)(2,1)} custom-call(s32[16]{0:T(128)} %lens.1, s32[128]{0:T(128)} %dest.1, bf16[4,128,4352]{2,1,0:T(8,128)(2,1)} %bitcast.5, bf16[64,512]{1,0:T(8,128)(2,1)} %bitcast.6, f32[4,4352]{1,0:T(4,128)} %w_ref.1, f32[4352]{0:T(1024)} %b_ref.1, f32[1,64]{1,0:T(1,128)} %bitcast.7, f32[1,64]{1,0:T(1,128)} %bitcast.8, ...), custom_call_target="tpu_custom_call" | custom-call | flops 2000000000 | bytes 10000000 | tf_op jit(solution)/shard_map/pallas_call | solution.py:555
  138.5 3.3 %shard_map.92 = bf16[512,4096]{1,0:T(8,128)(2,1)} custom-call(bf16[512,4096]{1,0:T(8,128)(2,1)} %shard_map.91.source), custom_call_target="tpu_custom_call" | custom-call | tf_op jit(solution)/shard_map/pallas_call | solution.py:569
